TPU v7x, 32 devices: a whole 2x2x4 slice. The times are simulated.
32 devices in a mesh: loop: 8 (over y, x, core), stack: 4 (over z).
Axes of the slice: x: 2, y: 2, z: 4, core: 2. Of those that a mesh axis runs over, the one named last changes fastest.
Arguments:
- spectra: bfloat16 [512, 2, 32, 1024], P('stack', None, None, 'loop'), may hold values from -6 to 6
- channel_loc: int32 [1024], P('loop'), may hold values from 0 to 2047, as said below
- channel_valid: int32 [1024], P('loop'), may hold values 0 or 1
- bin_owner: int32 [32], replicated, may hold values from 0 to 3, as said below
Outputs:
- linear_stack: float32 [4, 16, 1024], P('stack', 'loop')
- phase_stack: float32 [4, 16, 1024], P('stack', 'loop')
Inputs may be any that keep to these rules, and one draw needn't show every extreme that they name: `channel_loc`: strictly increasing along the channels; channel c lies at 2 c or 2 c + 1, the first at 0 and the last at 2047. `bin_owner`: at most 16 bins share an owner; some owner holds exactly 16.
All inputs are finite; a program needn't handle non-finite values. No bound on the sum of `channel_valid` on one device may be relied on, other than what follows from the above.
Results may differ from a plain program's by a relative error of at most 0.003.
Values may be sent and summed in bfloat16 or wider, within the bound.
A program may use at most 128 MiB of HBM per device.

v0:
```python
import functools
import math

import jax
import jax.numpy as jnp
import numpy as np
from jax import lax
from jax.experimental import pallas as pl
from jax.experimental.pallas import tpu as pltpu
from jax.sharding import PartitionSpec as P

BCAP = 16
LANES = 128


def lag_matrix(freq_count):
    freq_ids = np.arange(freq_count)
    lag_ids = np.arange(2 * freq_count) - freq_count
    turns = freq_ids[:, None] * lag_ids[None, :] % (2 * freq_count)
    angle = turns * (math.pi / freq_count)
    bin_weight = np.where(freq_ids == 0, 1.0, 2.0)[:, None]
    return np.concatenate(
        [bin_weight * np.cos(angle), -bin_weight * np.sin(angle)], 0
    ).astype(np.float32)


def normalize(series):
    return series / jnp.sqrt(jnp.mean(series * series, axis=-1, keepdims=True) + 1e-06)


def finish(linear_re, linear_im, phase_re, phase_im):
    coherence = phase_re * phase_re + phase_im * phase_im
    matrix = jnp.asarray(lag_matrix(linear_re.shape[1]))
    rows = linear_re.shape[0]
    both = jnp.dot(
        jnp.concatenate(
            [
                jnp.concatenate([linear_re, linear_im], 1),
                jnp.concatenate([linear_re * coherence, linear_im * coherence], 1),
            ],
            0,
        ),
        matrix,
        precision=lax.Precision.HIGHEST,
    )
    both = normalize(both)
    return both[:rows], both[rows:]


def pair_kernel(bin_count, seg2, x_ref, perm_ref, keep_ref, shift_ref, out_ref, left, right):
    groups, freqs = x_ref.shape[0], x_ref.shape[1]
    half = seg2 // 2
    reps = LANES // bin_count

    def fold(block):
        total = block[:bin_count]
        for rep in range(1, reps):
            total = total + block[rep * bin_count : (rep + 1) * bin_count]
        return total

    right[...] = jnp.zeros_like(right)

    def freq_pair(pair, carry):
        rows = jnp.concatenate(
            [x_ref[g, pl.ds(2 * pair, 2)].reshape(2 * seg2, LANES) for g in range(groups)], 1
        )
        for block in range(groups):
            cols = jnp.dot(
                rows,
                perm_ref[:, block * LANES : (block + 1) * LANES],
                preferred_element_type=jnp.float32,
            )
            left[block * LANES : (block + 1) * LANES] = cols.T.astype(jnp.bfloat16)
            for which in range(2):
                at = which * seg2
                re, im = cols[at : at + half], cols[at + half : at + seg2]
                right[block, which, at : at + seg2, :LANES] = cols[at : at + seg2].astype(
                    jnp.bfloat16
                )
                right[block, which, at : at + seg2, LANES:] = jnp.concatenate(
                    [-im, re], 0
                ).astype(jnp.bfloat16)

        def one_freq(which, carry):
            def products(row_block, weights):
                lhs = left[pl.ds(pl.multiple_of(row_block * LANES, LANES), LANES)]
                both = jnp.dot(lhs, weights, preferred_element_type=jnp.float32)
                re, im = both[:, :LANES], both[:, LANES:]
                scale = lax.rsqrt(jnp.maximum(re * re + im * im, 1.0))
                return re, im, re * scale, im * scale

            zero = jnp.zeros((bin_count, LANES), jnp.float32)
            sums, moved = (zero,) * 4, (zero,) * 4
            for block in range(groups):
                weights = right[block, which]

                def add(row_block, sums):
                    parts = products(row_block, weights)
                    return tuple(s + fold(p) for s, p in zip(sums, parts))

                if groups <= 8:
                    for row_block in range(block):
                        sums = add(row_block, sums)
                else:
                    sums = lax.fori_loop(0, block, add, sums)
                parts = products(block, weights)
                keep, shift = keep_ref[block], shift_ref[block]
                sums = tuple(s + fold(p * keep) for s, p in zip(sums, parts))
                moved = tuple(s + fold(p * shift) for s, p in zip(moved, parts))
            for c in range(4):
                out_ref[2 * pair + which, c, 0] = sums[c]
                out_ref[2 * pair + which, c, 1] = moved[c]
            return carry

        return lax.fori_loop(0, 2, one_freq, carry)

    lax.fori_loop(0, freqs // 2, freq_pair, 0)


def on_device(spectra, channel_loc, channel_valid, bin_owner):
    loop_size = lax.axis_size("loop")
    stack_size = lax.axis_size("stack")
    freq_dev, _, seg, channels = spectra.shape
    bin_count = bin_owner.shape[0]
    groups = loop_size
    nch = groups * channels
    hop = nch // bin_count
    freqs = freq_dev // loop_size
    seg2 = 2 * seg
    reps = LANES // bin_count

    x = lax.all_to_all(
        spectra.reshape(loop_size, freqs, seg2, channels), "loop", 0, 0, tiled=True
    )
    table = lax.all_gather(jnp.stack([channel_loc, channel_valid]), "loop", axis=1, tiled=True)
    late = table[0] - 2 * jnp.arange(nch, dtype=jnp.int32)
    valid = table[1]

    chan = jnp.arange(nch, dtype=jnp.int32)
    place = (chan % hop) * bin_count + chan // hop
    perm = jnp.where(
        (place[:, None] == chan[None, :]) & (valid[:, None] > 0), 1.0, 0.0
    ).astype(jnp.bfloat16)
    late = late.reshape(bin_count, hop).T.reshape(groups, LANES)
    lane = jnp.arange(LANES, dtype=jnp.int32)
    rep, step = lane // bin_count, lane % bin_count
    same = (rep[:, None] == rep[None, :]) & (step[None, :] > step[:, None])
    early = late[:, None, :] < late[:, :, None]
    keep = ((rep[:, None] < rep[None, :])[None] | (same[None] & ~early)).astype(jnp.float32)
    shift = (same[None] & early).astype(jnp.float32)

    whole = pl.BlockSpec(memory_space=pltpu.VMEM)
    pair_sums = pl.pallas_call(
        functools.partial(pair_kernel, bin_count, seg2),
        out_shape=jax.ShapeDtypeStruct((freqs, 4, 2, bin_count, LANES), jnp.float32),
        in_specs=[whole] * 4,
        out_specs=whole,
        scratch_shapes=[
            pltpu.VMEM((nch, 2 * seg2), jnp.bfloat16),
            pltpu.VMEM((groups, 2, 2 * seg2, 2 * LANES), jnp.bfloat16),
        ],
        compiler_params=pltpu.CompilerParams(vmem_limit_bytes=48 * 2**20),
        cost_estimate=pl.CostEstimate(
            flops=freqs * nch * nch * seg2 * 2, bytes_accessed=8 * 2**20, transcendentals=0
        ),
    )(x, perm, keep, shift)

    gap = step[None, :] - jnp.arange(bin_count, dtype=jnp.int32)[:, None]
    labels = jnp.arange(bin_count, dtype=jnp.int32)
    ahead = gap[..., None] == labels
    behind = -gap[..., None] - 1 == labels
    below = (gap[..., None] - 1 == labels) & (gap[..., None] > 0)
    to_bin = jnp.stack(
        [jnp.stack([ahead, behind], 2), jnp.stack([below, jnp.zeros_like(below)], 2)], 0
    ).astype(jnp.float32)
    binned = jnp.dot(
        pair_sums.reshape(freqs * 4, 2 * bin_count * LANES),
        to_bin.reshape(2 * bin_count * LANES, 2 * bin_count),
        precision=lax.Precision.HIGHEST,
    ).reshape(freqs, 4, 2, bin_count)
    sign = jnp.array([1.0, -1.0, 1.0, -1.0], jnp.float32)[None, :, None]
    bins = binned[:, :, 0] + sign * binned[:, :, 1]

    same_owner = bin_owner[:, None] == bin_owner[None, :]
    earlier = labels[None, :] < labels[:, None]
    slot_rank = jnp.sum((same_owner & earlier).astype(jnp.int32), axis=1)
    slot = bin_owner * BCAP + slot_rank
    placement = (
        slot[:, None] == jnp.arange(BCAP * stack_size, dtype=jnp.int32)[None, :]
    ).astype(jnp.float32)
    packed = jnp.einsum("bs,fcb->scf", placement, bins, precision=lax.Precision.HIGHEST)
    devices = stack_size * loop_size
    packed = packed.reshape(devices, BCAP // loop_size, 4, freqs)
    owned = lax.all_to_all(packed, ("stack", "loop"), 0, 0, tiled=True)
    row_total = BCAP // loop_size
    sums = owned.transpose(1, 2, 0, 3).reshape(row_total, 4, devices * freqs)
    linear, weighted = finish(sums[:, 0], sums[:, 1], sums[:, 2], sums[:, 3])
    return (linear.reshape(1, row_total, -1), weighted.reshape(1, row_total, -1))


def solution(mesh):
    in_specs = (P("stack", None, None, "loop"), P("loop"), P("loop"), P())
    out_specs = (P("stack", "loop", None), P("stack", "loop", None))
    return jax.shard_map(
        on_device, mesh=mesh, in_specs=in_specs, out_specs=out_specs, check_vma=False
    )
```

profile of v0, /device:TPU:0, one launch (start us, length us, event | category | flops | bytes accessed | tf_op | source)
XLA Modules:
  0.0 93.2 jit_solution(11025086849471432501)
XLA Ops:
  0.6 5.2 %all-to-all-start = ((bf16[8,16,64,128]{3,2,1,0:T(8,128)(2,1)}), bf16[8,16,64,128]{3,2,1,0:T(8,128)(2,1)S(1)}, u32[]{:S(2)}, u32[]{:S(2)}) async-start(bf16[8,16,64,128]{3,2,1,0:T(8,128)(2,1)} %bitcast.71), calls=%async_computation | async-start | bytes 4194304 | tf_op jit(solution)/shard_map/all_to_all | solution.py:132
  5.8 0.0 copy-start.3
  5.8 0.0 copy-start.4
  5.9 0.1 fusion.3
  6.0 0.1 iota_compare_fusion.2
  6.3 1.3 %reshape.304 = pred[8192,64]{0,1:T(32,128)(4,1)} reshape(pred[2,32,128,2,32]{2,1,0,4,3:T(32,128)(4,1)S(1)} %pad_add_fusion) | data formatting | bytes 1048576 | tf_op jit(solution)/shard_map/reshape | solution.py:178
  7.5 0.0 copy-done.3
  7.6 27.9 %all_gather.3 = s32[2,1024]{1,0:T(2,128)S(1)} all-gather(s32[2,128]{1,0:T(2,128)S(1)} %pad_add_fusion.1), channel_id=1, replica_groups=mesh['loop'=8,'stack'=4] {'loop'}, dimensions={1}, use_global_device_ids=true | all-gather | bytes 9216 | tf_op jit(solution)/shard_map/all_gather | solution.py:135
  35.5 0.1 squeeze.17
  35.6 0.1 copy.28
  35.7 0.1 lt.78
  35.8 0.2 convert_reduce_fusion
  36.0 0.1 broadcast_compare_fusion
  36.1 0.2 fusion.7
  36.3 2.1 %select_convert_fusion.perm_ref = bf16[1024,1024]{1,0:T(8,128)(2,1)} fusion(s32[1024]{0:T(1024)S(1)} %fusion.25, pred[1024]{0:T(1024)(128)(4,1)S(1)} %compare_reduce_fusion), kind=kLoop, calls=%fused_computation | loop fusion | flops 4194304 | bytes 2102272 | tf_op jit(solution)/shard_map/convert_element_type | solution.py:143
  38.5 0.0 all-to-all-done.x_ref
  38.5 29.5 %shard_map.77 = f32[16,4,2,32,128]{4,3,2,1,0:T(8,128)S(1)} custom-call(bf16[8,16,64,128]{3,2,1,0:T(8,128)(2,1)S(1)} %all-to-all-done.x_ref, bf16[1024,1024]{1,0:T(8,128)(2,1)} %select_convert_fusion.perm_ref, f32[8,128,128]{2,1,0:T(8,128)S(1)} %get-tuple-element.3.keep_ref, f32[8,128,128]{2,1,0:T(8,128)S(1)} %get-tuple-element.2.shift_ref), custom_call_target="tpu_custom_call" | custom-call | flops 2147483648 | bytes 8388608 | tf_op jit(solution)/shard_map/pallas_call | solution.py:153
  68.0 1.3 %copy-done = f32[16,4,2,32,128]{4,3,2,1,0:T(8,128)} copy-done((f32[16,4,2,32,128]{4,3,2,1,0:T(8,128)}, f32[16,4,2,32,128]{4,3,2,1,0:T(8,128)S(1)}, u32[]{:S(2)}) %copy-start) | copy-done | bytes 2097176
  69.4 2.1 %dot_general.15 = f32[16,4,8192]{2,1,0:T(4,128)S(1)} reshape(f32[16,4,2,32,128]{4,3,2,1,0:T(8,128)} %copy-done) | data formatting | bytes 4194304 | tf_op jit(solution)/shard_map/dot_general | solution.py:176
  71.5 0.0 copy-start.5
  71.5 3.4 %fusion.1 = f32[16,4,2,32]{3,0,2,1:T(8,128)S(1)} fusion(pred[2,32,8192,1]{2,1,0,3:T(32,128)(4,1)S(1)} %bitcast.70, f32[16,4,8192,1]{2,1,0,3:T(4,128)S(1)} %bitcast.69), kind=kOutput, calls=%fused_computation.3 | convolution fusion | flops 402653184 | bytes 2637824 | tf_op jit(solution)/shard_map/dot_general | solution.py:176
  75.0 0.2 convolution_bitcast_fusion
  75.2 0.1 copy.31
  75.4 0.2 reshape.320
  75.5 10.9 %all_to_all.10 = f32[32,1,128]{2,1,0:T(1,128)S(1)} all-to-all(f32[32,1,128]{2,1,0:T(1,128)S(1)} %reshape.320), channel_id=1, replica_groups=mesh['loop'=8,'stack'=4] {'stack','loop'}, dimensions={0} | all-to-all | bytes 32768 | tf_op jit(solution)/shard_map/all_to_all | solution.py:194
  86.5 0.5 broadcast.341
  87.0 0.7 reduce.6
  87.7 0.2 reshape.321
  88.0 0.1 reshape.306
  88.1 4.4 %multiply_reduce_fusion = (f32[4]{0:T(128)S(1)}, f32[4,1024]{1,0:T(4,128)S(1)}) fusion(f32[1024,1024]{1,0:T(8,128)} %constant.84.clone, f32[2,512]{1,0:T(2,128)S(1)} %get-tuple-element.10, f32[2,512]{1,0:T(2,128)S(1)} %get-tuple-element.9, f32[2,512]{1,0:T(2,128)S(1)} %bitcast.74, f32[2,512]{1,0:T(2,128)S(1)} %bitcast.75), kind=kOutput, calls=%fused_computation.26 | convolution fusion | flops 50352124 | bytes 4227088 | tf_op jit(solution)/shard_map/dot_general | solution.py:35
  92.5 0.1 broadcast_divide_fusion
  92.6 0.6 slice_bitcast_fusion.3
  (28 shorter events, 0.3 us)
Async XLA Ops:
  0.6 37.8 %all-to-all-start = ((bf16[8,16,64,128]{3,2,1,0:T(8,128)(2,1)}), bf16[8,16,64,128]{3,2,1,0:T(8,128)(2,1)S(1)}, u32[]{:S(2)}, u32[]{:S(2)}) async-start(bf16[8,16,64,128]{3,2,1,0:T(8,128)(2,1)} %bitcast.71), calls=%async_computation | async-start | bytes 4194304 | tf_op jit(solution)/shard_map/all_to_all | solution.py:132
  5.8 1.7 %copy-start.2 = (s32[128]{0:T(128)S(1)}, s32[128]{0:T(128)}, u32[]{:S(2)}) copy-start(s32[128]{0:T(128)} %param.8) | copy-start | bytes 1540
  5.8 1.7 %copy-start.3 = (s32[128]{0:T(128)S(1)}, s32[128]{0:T(128)}, u32[]{:S(2)}) copy-start(s32[128]{0:T(128)} %param.7) | copy-start | bytes 1540
  5.8 29.9 %copy-start.4 = (s32[32]{0:T(128)S(1)}, s32[32]{0:T(128)}, u32[]{:S(2)}) copy-start(s32[32]{0:T(128)} %param.9) | copy-start | bytes 388
  68.0 1.3 %copy-start = (f32[16,4,2,32,128]{4,3,2,1,0:T(8,128)}, f32[16,4,2,32,128]{4,3,2,1,0:T(8,128)S(1)}, u32[]{:S(2)}) copy-start(f32[16,4,2,32,128]{4,3,2,1,0:T(8,128)S(1)} %shard_map.77) | copy-start | bytes 6291460
  69.4 2.2 %copy-start.1 = (pred[8192,64]{0,1:T(32,128)(4,1)S(1)}, pred[8192,64]{0,1:T(32,128)(4,1)}, u32[]{:S(2)}) copy-start(pred[8192,64]{0,1:T(32,128)(4,1)} %reshape.304) | copy-start | bytes 1572868
  71.5 3.5 %copy-start.5 = (f32[4]{0:T(128)S(1)}, f32[4]{0:T(128)}, u32[]{:S(2)}) copy-start(f32[4]{0:T(128)} %constant.83.clone) | copy-start | bytes 52
where the time goes:
time: 93.6 us; the launch traced here: 93.2 us
  blocking collectives  38.9 us (42%)
  Pallas kernels  29.5 us (32%)
  matrix products  8.03 us (9%)
  local copies, waits for them, and re-layouts  6.92 us (7%)
  starting transfers between devices  5.18 us (6%)
  other arithmetic  3.81 us (4%)
    pallas_call x1, Pallas kernels, on_device(): pl.pallas_call(functools.partial(pair_kernel, bin_count, seg2), out_shape...  29.5 us
    all_gather x1, blocking collectives, on_device(): lax.all_gather(jnp.stack([channel_loc, channel_valid]), 'loop', axis=1, t...  27.9 us
    all_to_all x1, blocking collectives, on_device(): owned = lax.all_to_all(packed, ('stack', 'loop'), 0, 0, tiled=True)  10.9 us
    all_to_all x1, starting transfers between devices, on_device(): lax.all_to_all(spectra.reshape(loop_size, freqs, seg2, channels), 'loop',...  5.18 us
    dot_general x1, matrix products, finish(): jnp.dot(jnp.concatenate([jnp.concatenate([linear_re, linear_im], 1), jnp....  4.38 us
    dot_general x1, matrix products, on_device(): jnp.dot(pair_sums.reshape(freqs * 4, 2 * bin_count * LANES), to_bin.resha...  3.43 us
    dot_general x1, local copies, waits for them, and re-layouts, on_device(): jnp.dot(pair_sums.reshape(freqs * 4, 2 * bin_count * LANES), to_bin.resha...  2.15 us
    convert_element_type x1, other arithmetic, on_device(): perm = jnp.where((place[:, None] == chan[None, :]) & (valid[:, None] > 0)...  2.15 us
  transfers between devices with their start and end apart: 1, of which 0 were waited for; matrix products, arithmetic and copies ran while one was open for 5% of the time, Pallas kernels for 0%

commit v1 on v0

--- a/solution.py
+++ b/solution.py
@@ -47,10 +47,78 @@
     return both[:rows], both[rows:]
 
 
-def pair_kernel(bin_count, seg2, x_ref, perm_ref, keep_ref, shift_ref, out_ref, left, right):
+def pair_kernel(
+    bin_count,
+    seg2,
+    spectra_ref,
+    table_ref,
+    perm_hbm,
+    base_ref,
+    out_ref,
+    x_ref,
+    tables,
+    perm_ref,
+    keep_ref,
+    shift_ref,
+    left,
+    right,
+    send_sem,
+    recv_sem,
+    table_send,
+    table_recv,
+    local_sem,
+):
     groups, freqs = x_ref.shape[0], x_ref.shape[1]
     half = seg2 // 2
     reps = LANES // bin_count
+    me = lax.axis_index("loop")
+
+    def peer(k):
+        return lax.rem(me + k, groups)
+
+    own = pltpu.make_async_copy(spectra_ref.at[me], x_ref.at[me], local_sem.at[0])
+    own.start()
+    fetch = pltpu.make_async_copy(perm_hbm, perm_ref, local_sem.at[1])
+    fetch.start()
+    own_table = pltpu.make_async_copy(table_ref, tables.at[me], local_sem.at[2])
+    own_table.start()
+
+    barrier = pltpu.get_barrier_semaphore()
+    for k in range(1, groups):
+        pl.semaphore_signal(
+            barrier, inc=1, device_id={"loop": peer(k)}, device_id_type=pl.DeviceIdType.MESH
+        )
+    pl.semaphore_wait(barrier, groups - 1)
+
+    def table_copy(k):
+        return pltpu.make_async_remote_copy(
+            src_ref=table_ref,
+            dst_ref=tables.at[me],
+            send_sem=table_send.at[k - 1],
+            recv_sem=table_recv.at[k - 1],
+            device_id={"loop": peer(k)},
+            device_id_type=pl.DeviceIdType.MESH,
+        )
+
+    def pair_copy(pair, k):
+        return pltpu.make_async_remote_copy(
+            src_ref=spectra_ref.at[peer(k), pl.ds(2 * pair, 2)],
+            dst_ref=x_ref.at[me, pl.ds(2 * pair, 2)],
+            send_sem=send_sem.at[pair, k - 1],
+            recv_sem=recv_sem.at[pair, k - 1],
+            device_id={"loop": peer(k)},
+            device_id_type=pl.DeviceIdType.MESH,
+        )
+
+    for k in range(1, groups):
+        table_copy(k).start()
+
+    def send_pair(pair, carry):
+        for k in range(1, groups):
+            pair_copy(pair, k).start()
+        return carry
+
+    lax.fori_loop(0, freqs // 2, send_pair, 0)
 
     def fold(block):
         total = block[:bin_count]
@@ -59,11 +127,47 @@
         return total
 
     right[...] = jnp.zeros_like(right)
+    fetch.wait()
+    own_table.wait()
+    for k in range(1, groups):
+        table_copy(k).wait()
+    flags = jnp.concatenate([tables[g] for g in range(groups)], 1).astype(jnp.float32)
+    valid = flags[1:2].astype(jnp.bfloat16)
+    flags = flags.astype(jnp.bfloat16)
+    for block in range(groups):
+        late = jnp.dot(
+            flags,
+            perm_ref[:, block * LANES : (block + 1) * LANES],
+            preferred_element_type=jnp.float32,
+        )[0:1]
+        late = jnp.broadcast_to(late, (LANES, LANES))
+        early = late.T * (1.0 - late)
+        keep_ref[block] = base_ref[0] + base_ref[1] * (1.0 - early)
+        shift_ref[block] = base_ref[1] * early
+    own.wait()
+
+    row_ids = lax.broadcasted_iota(jnp.int32, (bin_count, LANES), 0)
+    lane_ids = lax.broadcasted_iota(jnp.int32, (bin_count, LANES), 1)
+    ahead = row_ids <= (lane_ids & (bin_count - 1))
+
+    sub_ids = row_ids[:8]
+
+    def turn(part):
+        count = bin_count
+        while count > 8:
+            count //= 2
+            part = part[:count] + pltpu.roll(part[count:], LANES - count, 1)
+        for step in (4, 2, 1):
+            part = jnp.where((sub_ids & step) != 0, pltpu.roll(part, LANES - step, 1), part)
+        return part
 
     def freq_pair(pair, carry):
+        for k in range(1, groups):
+            pair_copy(pair, k).wait_recv()
         rows = jnp.concatenate(
             [x_ref[g, pl.ds(2 * pair, 2)].reshape(2 * seg2, LANES) for g in range(groups)], 1
         )
+        rows = rows * valid
         for block in range(groups):
             cols = jnp.dot(
                 rows,
@@ -108,13 +212,25 @@
                 sums = tuple(s + fold(p * keep) for s, p in zip(sums, parts))
                 moved = tuple(s + fold(p * shift) for s, p in zip(moved, parts))
             for c in range(4):
-                out_ref[2 * pair + which, c, 0] = sums[c]
-                out_ref[2 * pair + which, c, 1] = moved[c]
+                both = (
+                    jnp.where(ahead, sums[c], 0.0),
+                    jnp.where(ahead, 0.0, sums[c]),
+                    moved[c],
+                )
+                for n, part in enumerate(both):
+                    out_ref[2 * pair + which, 3 * c + n] = jnp.sum(turn(part), axis=0)
             return carry
 
         return lax.fori_loop(0, 2, one_freq, carry)
 
     lax.fori_loop(0, freqs // 2, freq_pair, 0)
+
+    def sent(pair, carry):
+        for k in range(1, groups):
+            pair_copy(pair, k).wait_send()
+        return carry
+
+    lax.fori_loop(0, freqs // 2, sent, 0)
 
 
 def on_device(spectra, channel_loc, channel_valid, bin_owner):
@@ -129,53 +245,63 @@
     seg2 = 2 * seg
     reps = LANES // bin_count
 
-    x = lax.all_to_all(
-        spectra.reshape(loop_size, freqs, seg2, channels), "loop", 0, 0, tiled=True
-    )
-    table = lax.all_gather(jnp.stack([channel_loc, channel_valid]), "loop", axis=1, tiled=True)
-    late = table[0] - 2 * jnp.arange(nch, dtype=jnp.int32)
-    valid = table[1]
-
-    chan = jnp.arange(nch, dtype=jnp.int32)
+    x = spectra.reshape(loop_size, freqs, seg2, channels)
+    first = lax.axis_index("loop") * channels
+    late = channel_loc - 2 * (first + jnp.arange(channels, dtype=jnp.int32))
+    table = jnp.pad(jnp.stack([late, channel_valid]), ((0, 6), (0, 0)))
+
+    chan = np.arange(nch)
     place = (chan % hop) * bin_count + chan // hop
-    perm = jnp.where(
-        (place[:, None] == chan[None, :]) & (valid[:, None] > 0), 1.0, 0.0
-    ).astype(jnp.bfloat16)
-    late = late.reshape(bin_count, hop).T.reshape(groups, LANES)
-    lane = jnp.arange(LANES, dtype=jnp.int32)
+    perm = jnp.asarray(place[:, None] == chan[None, :], jnp.bfloat16)
+    lane = np.arange(LANES)
     rep, step = lane // bin_count, lane % bin_count
     same = (rep[:, None] == rep[None, :]) & (step[None, :] > step[:, None])
-    early = late[:, None, :] < late[:, :, None]
-    keep = ((rep[:, None] < rep[None, :])[None] | (same[None] & ~early)).astype(jnp.float32)
-    shift = (same[None] & early).astype(jnp.float32)
+    base = jnp.asarray(np.stack([rep[:, None] < rep[None, :], same]), jnp.float32)
 
     whole = pl.BlockSpec(memory_space=pltpu.VMEM)
+    far = pl.BlockSpec(memory_space=pl.ANY)
     pair_sums = pl.pallas_call(
         functools.partial(pair_kernel, bin_count, seg2),
-        out_shape=jax.ShapeDtypeStruct((freqs, 4, 2, bin_count, LANES), jnp.float32),
-        in_specs=[whole] * 4,
+        out_shape=jax.ShapeDtypeStruct((freqs, 12, LANES), jnp.float32),
+        in_specs=[far, whole, far, whole],
         out_specs=whole,
         scratch_shapes=[
+            pltpu.VMEM((loop_size, freqs, seg2, channels), jnp.bfloat16),
+            pltpu.VMEM((loop_size, 8, LANES), jnp.int32),
+            pltpu.VMEM((nch, nch), jnp.bfloat16),
+            pltpu.VMEM((groups, LANES, LANES), jnp.float32),
+            pltpu.VMEM((groups, LANES, LANES), jnp.float32),
             pltpu.VMEM((nch, 2 * seg2), jnp.bfloat16),
             pltpu.VMEM((groups, 2, 2 * seg2, 2 * LANES), jnp.bfloat16),
+            pltpu.SemaphoreType.DMA((freqs // 2, groups - 1)),
+            pltpu.SemaphoreType.DMA((freqs // 2, groups - 1)),
+            pltpu.SemaphoreType.DMA((groups - 1,)),
+            pltpu.SemaphoreType.DMA((groups - 1,)),
+            pltpu.SemaphoreType.DMA((3,)),
         ],
-        compiler_params=pltpu.CompilerParams(vmem_limit_bytes=48 * 2**20),
+        compiler_params=pltpu.CompilerParams(
+            vmem_limit_bytes=48 * 2**20, collective_id=0, has_side_effects=True
+        ),
         cost_estimate=pl.CostEstimate(
             flops=freqs * nch * nch * seg2 * 2, bytes_accessed=8 * 2**20, transcendentals=0
         ),
-    )(x, perm, keep, shift)
-
-    gap = step[None, :] - jnp.arange(bin_count, dtype=jnp.int32)[:, None]
+    )(x, table, perm, base)
+
     labels = jnp.arange(bin_count, dtype=jnp.int32)
-    ahead = gap[..., None] == labels
-    behind = -gap[..., None] - 1 == labels
-    below = (gap[..., None] - 1 == labels) & (gap[..., None] > 0)
-    to_bin = jnp.stack(
-        [jnp.stack([ahead, behind], 2), jnp.stack([below, jnp.zeros_like(below)], 2)], 0
-    ).astype(jnp.float32)
+    col = np.arange(LANES)[:, None] % bin_count
+    row = np.arange(bin_count)[None, :]
+    none = np.zeros((LANES, bin_count))
+    to_bin = np.concatenate(
+        [
+            np.concatenate([col == row, none], 1),
+            np.concatenate([none, col == bin_count - 1 - row], 1),
+            np.concatenate([col - 1 == row, none], 1),
+        ],
+        0,
+    ).astype(np.float32)
     binned = jnp.dot(
-        pair_sums.reshape(freqs * 4, 2 * bin_count * LANES),
-        to_bin.reshape(2 * bin_count * LANES, 2 * bin_count),
+        pair_sums.reshape(freqs * 4, 3 * LANES),
+        jnp.asarray(to_bin),
         precision=lax.Precision.HIGHEST,
     ).reshape(freqs, 4, 2, bin_count)
     sign = jnp.array([1.0, -1.0, 1.0, -1.0], jnp.float32)[None, :, None]

time: 93.6 us -> 70.9 us (0.76)
  blocking collectives: 38.9 us -> 13 us
  Pallas kernels: 29.5 us -> 43.6 us
  starting transfers between devices: 5.18 us -> 0 us
  matrix products: 8.03 us -> 5.04 us
  other arithmetic: 3.81 us -> 2.3 us
  local copies, waits for them, and re-layouts: 6.92 us -> 5.98 us
    all_gather x1 -> x0, blocking collectives: 27.9 us -> none  [on_device(): lax.all_gather(jnp.stack([channel_loc, channel_valid]), 'loop', axis=1, t...]
    pallas_call x1, Pallas kernels: 29.5 us -> 43.6 us  [on_device(): pl.pallas_call(functools.partial(pair_kernel, bin_count, seg2), out_shape...]
    all_to_all x1 -> x0, starting transfers between devices: 5.18 us -> none  [on_device(): lax.all_to_all(spectra.reshape(loop_size, freqs, seg2, channels), 'loop',...]
    dot_general x1, matrix products: 3.43 us -> 0.45 us  [on_device(): jnp.dot(pair_sums.reshape(freqs * 4, 3 * LANES), jnp.asarray(to_bin), pre...]
    unnamed x16 -> x14, local copies, waits for them, and re-layouts: 1.77 us -> 4.49 us
    convert_element_type x2 -> x0, other arithmetic: 2.36 us -> none  [the longest x1 2.15 us: on_device(): perm = jnp.where((place[:, None] == chan[None, :]) & (valid[:, None] > 0)...]
    dot_general x1, local copies, waits for them, and re-layouts: 2.15 us -> 0.04 us  [on_device(): jnp.dot(pair_sums.reshape(freqs * 4, 3 * LANES), jnp.asarray(to_bin), pre...]
    all_to_all x1, blocking collectives: 10.9 us -> 13 us  [on_device(): owned = lax.all_to_all(packed, ('stack', 'loop'), 0, 0, tiled=True)]
  transfers between devices with their start and end apart: 1 -> 0, of which waited for: 0 -> 0; matrix products, arithmetic and copies ran while one was open for 5% -> 0% of each run, Pallas kernels for 0% -> 0%
where the time goes in v1:
time: 70.9 us; the launch traced here: 70.7 us
  Pallas kernels  43.6 us (61%)
  blocking collectives  13 us (18%)
  local copies, waits for them, and re-layouts  5.98 us (8%)
  matrix products  5.04 us (7%)
  other arithmetic  2.3 us (3%)
  between operations  0.78 us (1%)
    pallas_call x1, Pallas kernels, on_device(): pl.pallas_call(functools.partial(pair_kernel, bin_count, seg2), out_shape...  43.6 us
    all_to_all x1, blocking collectives, on_device(): owned = lax.all_to_all(packed, ('stack', 'loop'), 0, 0, tiled=True)  13 us
    unnamed x14, local copies, waits for them, and re-layouts  4.49 us
    dot_general x1, matrix products, finish(): jnp.dot(jnp.concatenate([jnp.concatenate([linear_re, linear_im], 1), jnp....  4.38 us

profile of v1, /device:TPU:0, one launch (start us, length us, event | category | flops | bytes accessed | tf_op | source)
XLA Modules:
  0.0 70.7 jit_solution(9704060481521929472)
XLA Ops:
  0.6 0.0 copy-start.4
  0.6 0.7 subtract_bitcast_fusion
  1.3 0.7 pad_add_fusion
  2.0 0.0 copy-start
  2.0 1.6 %copy-done = bf16[128,2,32,128]{3,2,1,0:T(8,128)(2,1)S(1)} copy-done((bf16[128,2,32,128]{3,2,1,0:T(8,128)(2,1)S(1)}, bf16[128,2,32,128]{3,2,1,0:T(8,128)(2,1)}, u32[]{:S(2)}) %copy-start) | copy-done | bytes 2097176
  3.6 0.0 copy-start.1
  3.6 1.6 %copy-done.1 = bf16[1024,1024]{1,0:T(8,128)(2,1)S(1)} copy-done((bf16[1024,1024]{1,0:T(8,128)(2,1)S(1)}, bf16[1024,1024]{1,0:T(8,128)(2,1)}, u32[]{:S(2)}) %copy-start.1) | copy-done | bytes 2097176
  5.2 0.0 copy-start.2
  5.2 0.9 %copy-done.2 = f32[2,128,128]{2,1,0:T(8,128)S(1)} copy-done((f32[2,128,128]{2,1,0:T(8,128)S(1)}, f32[2,128,128]{2,1,0:T(8,128)}, u32[]{:S(2)}) %copy-start.2) | copy-done | bytes 131096
  6.1 0.0 copy-start.3
  6.1 0.0 copy-start.5
  6.1 43.6 %shard_map.104 = f32[16,12,128]{2,1,0:T(8,128)S(1)} custom-call(bf16[8,16,64,128]{3,2,1,0:T(8,128)(2,1)S(1)} %bitcast.52, s32[8,128]{1,0:T(8,128)S(1)} %pad.4.table_ref, bf16[1024,1024]{1,0:T(8,128)(2,1)S(1)} %copy-done.1, f32[2,128,128]{2,1,0:T(8,128)S(1)} %copy-done.2), custom_call_target="tpu_custom_call" | custom-call | flops 2147483648 | bytes 8388608 | tf_op jit(solution)/shard_map/pallas_call | solution.py:263
  49.7 0.0 copy-done.4
  49.7 0.2 convert_reduce_fusion
  49.9 0.0 copy-done.3
  49.9 0.5 fusion
  50.4 0.0 copy-done.5
  50.4 0.2 convolution_bitcast_fusion
  50.6 0.1 copy.30
  50.8 0.2 reshape.47
  51.0 13.0 %all_to_all.5 = f32[32,1,128]{2,1,0:T(1,128)S(1)} all-to-all(f32[32,1,128]{2,1,0:T(1,128)S(1)} %reshape.47), channel_id=1, replica_groups=mesh['loop'=8,'stack'=4] {'stack','loop'}, dimensions={0} | all-to-all | bytes 32768 | tf_op jit(solution)/shard_map/all_to_all | solution.py:320
  63.9 0.5 broadcast.27
  64.4 0.7 reduce
  65.1 0.2 reshape.48
  65.4 0.1 reshape.41
  65.6 4.4 %multiply_reduce_fusion = (f32[4]{0:T(128)S(1)}, f32[4,1024]{1,0:T(4,128)S(1)}) fusion(f32[1024,1024]{1,0:T(8,128)} %constant.35.clone, f32[2,512]{1,0:T(2,128)S(1)} %get-tuple-element.8, f32[2,512]{1,0:T(2,128)S(1)} %get-tuple-element.7, f32[2,512]{1,0:T(2,128)S(1)} %get-tuple-element.11, f32[2,512]{1,0:T(2,128)S(1)} %get-tuple-element.12), kind=kOutput, calls=%fused_computation.8 | convolution fusion | flops 50352124 | bytes 4227088 | tf_op jit(solution)/shard_map/dot_general | solution.py:35
  70.0 0.1 broadcast_divide_fusion
  70.0 0.6 slice_bitcast_fusion.3
  (10 shorter events, 0.2 us)
Async XLA Ops:
  0.6 49.1 %copy-start.4 = (s32[32]{0:T(128)S(1)}, s32[32]{0:T(128)}, u32[]{:S(2)}) copy-start(s32[32]{0:T(128)} %param.12) | copy-start | bytes 388
  2.0 1.6 %copy-start = (bf16[128,2,32,128]{3,2,1,0:T(8,128)(2,1)S(1)}, bf16[128,2,32,128]{3,2,1,0:T(8,128)(2,1)}, u32[]{:S(2)}) copy-start(bf16[128,2,32,128]{3,2,1,0:T(8,128)(2,1)} %param.9) | copy-start | bytes 6291460
  3.6 1.6 %copy-start.1 = (bf16[1024,1024]{1,0:T(8,128)(2,1)S(1)}, bf16[1024,1024]{1,0:T(8,128)(2,1)}, u32[]{:S(2)}) copy-start(bf16[1024,1024]{1,0:T(8,128)(2,1)} %constant.31.clone.perm_hbm) | copy-start | bytes 6291460
  5.2 0.9 %copy-start.2 = (f32[2,128,128]{2,1,0:T(8,128)S(1)}, f32[2,128,128]{2,1,0:T(8,128)}, u32[]{:S(2)}) copy-start(f32[2,128,128]{2,1,0:T(8,128)} %constant.32.clone.base_ref) | copy-start | bytes 393220
  6.1 43.9 %copy-start.3 = (f32[2,32,384,1]{2,1,0,3:T(8,128)S(1)}, f32[2,32,384,1]{2,1,0,3:T(8,128)}, u32[]{:S(2)}) copy-start(f32[2,32,384,1]{2,1,0,3:T(8,128)} %constant.40) | copy-start | bytes 294916
  6.1 44.3 %copy-start.5 = (f32[4]{0:T(128)S(1)}, f32[4]{0:T(128)}, u32[]{:S(2)}) copy-start(f32[4]{0:T(128)} %constant.34.clone) | copy-start | bytes 52

commit v2 on v1

--- a/solution.py
+++ b/solution.py
@@ -24,37 +24,45 @@
     ).astype(np.float32)
 
 
-def normalize(series):
-    return series / jnp.sqrt(jnp.mean(series * series, axis=-1, keepdims=True) + 1e-06)
-
-
-def finish(linear_re, linear_im, phase_re, phase_im):
-    coherence = phase_re * phase_re + phase_im * phase_im
-    matrix = jnp.asarray(lag_matrix(linear_re.shape[1]))
-    rows = linear_re.shape[0]
-    both = jnp.dot(
-        jnp.concatenate(
-            [
-                jnp.concatenate([linear_re, linear_im], 1),
-                jnp.concatenate([linear_re * coherence, linear_im * coherence], 1),
-            ],
-            0,
-        ),
-        matrix,
-        precision=lax.Precision.HIGHEST,
+def thirds(value):
+    high = value.astype(jnp.bfloat16)
+    rest = value - high.astype(jnp.float32)
+    middle = rest.astype(jnp.bfloat16)
+    low = (rest - middle.astype(jnp.float32)).astype(jnp.bfloat16)
+    return high, middle, low
+
+
+def exact_dot(value, matrix, contract):
+    return sum(
+        lax.dot_general(
+            part, matrix, ((contract[0], contract[1]), ((), ())),
+            preferred_element_type=jnp.float32,
+        )
+        for part in thirds(value)
     )
-    both = normalize(both)
-    return both[:rows], both[rows:]
 
 
 def pair_kernel(
     bin_count,
     seg2,
+    ahead_tiles,
     spectra_ref,
-    table_ref,
+    loc_ref,
+    valid_ref,
     perm_hbm,
     base_ref,
-    out_ref,
+    to_bin_ref,
+    place_ref,
+    lag_hbm,
+    linear_ref,
+    weighted_ref,
+    table_ref,
+    part_sums,
+    packed,
+    shares,
+    owned,
+    lag_ref,
+    series,
     x_ref,
     tables,
     perm_ref,
@@ -66,15 +74,31 @@
     recv_sem,
     table_send,
     table_recv,
+    share_send,
+    share_recv,
+    owned_send,
+    owned_recv,
     local_sem,
 ):
     groups, freqs = x_ref.shape[0], x_ref.shape[1]
     half = seg2 // 2
     reps = LANES // bin_count
     me = lax.axis_index("loop")
+    floor = lax.axis_index("stack")
+    floors = owned.shape[0]
+    tile_rows = owned.shape[1]
+    freq_dev = groups * freqs
 
     def peer(k):
         return lax.rem(me + k, groups)
+
+    def above(k):
+        return lax.rem(floor + k, floors)
+
+    first = me * LANES + lax.broadcasted_iota(jnp.int32, (1, LANES), 1)
+    table_ref[...] = jnp.zeros_like(table_ref)
+    table_ref[0:1] = loc_ref[...] - 2 * first
+    table_ref[1:2] = valid_ref[...]
 
     own = pltpu.make_async_copy(spectra_ref.at[me], x_ref.at[me], local_sem.at[0])
     own.start()
@@ -88,7 +112,11 @@
         pl.semaphore_signal(
             barrier, inc=1, device_id={"loop": peer(k)}, device_id_type=pl.DeviceIdType.MESH
         )
-    pl.semaphore_wait(barrier, groups - 1)
+    for k in range(1, floors):
+        pl.semaphore_signal(
+            barrier, inc=1, device_id={"stack": above(k)}, device_id_type=pl.DeviceIdType.MESH
+        )
+    pl.semaphore_wait(barrier, groups + floors - 2)
 
     def table_copy(k):
         return pltpu.make_async_remote_copy(
@@ -118,7 +146,9 @@
             pair_copy(pair, k).start()
         return carry
 
-    lax.fori_loop(0, freqs // 2, send_pair, 0)
+    pairs = freqs // 2
+    lax.fori_loop(0, min(ahead_tiles, pairs), send_pair, 0)
+    fetch_lag = pltpu.make_async_copy(lag_hbm, lag_ref, local_sem.at[3])
 
     def fold(block):
         total = block[:bin_count]
@@ -127,6 +157,7 @@
         return total
 
     right[...] = jnp.zeros_like(right)
+    part_sums[...] = jnp.zeros_like(part_sums)
     fetch.wait()
     own_table.wait()
     for k in range(1, groups):
@@ -145,6 +176,7 @@
         keep_ref[block] = base_ref[0] + base_ref[1] * (1.0 - early)
         shift_ref[block] = base_ref[1] * early
     own.wait()
+    fetch_lag.start()
 
     row_ids = lax.broadcasted_iota(jnp.int32, (bin_count, LANES), 0)
     lane_ids = lax.broadcasted_iota(jnp.int32, (bin_count, LANES), 1)
@@ -162,6 +194,10 @@
         return part
 
     def freq_pair(pair, carry):
+        @pl.when(pair + ahead_tiles < pairs)
+        def _():
+            send_pair(pair + ahead_tiles, 0)
+
         for k in range(1, groups):
             pair_copy(pair, k).wait_recv()
         rows = jnp.concatenate(
@@ -211,6 +247,7 @@
                 keep, shift = keep_ref[block], shift_ref[block]
                 sums = tuple(s + fold(p * keep) for s, p in zip(sums, parts))
                 moved = tuple(s + fold(p * shift) for s, p in zip(moved, parts))
+            spot = (floor * freq_dev + me * freqs + 2 * pair + which) % LANES
             for c in range(4):
                 both = (
                     jnp.where(ahead, sums[c], 0.0),
@@ -218,7 +255,9 @@
                     moved[c],
                 )
                 for n, part in enumerate(both):
-                    out_ref[2 * pair + which, 3 * c + n] = jnp.sum(turn(part), axis=0)
+                    part_sums[3 * c + n, pl.ds(spot, 1)] = jnp.sum(
+                        turn(part), axis=0, keepdims=True
+                    )
             return carry
 
         return lax.fori_loop(0, 2, one_freq, carry)
@@ -230,7 +269,82 @@
             pair_copy(pair, k).wait_send()
         return carry
 
-    lax.fori_loop(0, freqs // 2, sent, 0)
+    rows = jnp.concatenate([part_sums[n] for n in range(12)], 1)
+    bins = exact_dot(rows, to_bin_ref[...], ((1,), (0,)))
+    packed[...] = sum(
+        lax.dot_general(
+            place_ref[...], part, (((1,), (1,)), ((), ())), preferred_element_type=jnp.float32
+        )
+        for part in thirds(bins)
+    ).reshape(packed.shape)
+
+    def share_copy(k):
+        return pltpu.make_async_remote_copy(
+            src_ref=packed.at[peer(k)],
+            dst_ref=shares.at[me],
+            send_sem=share_send.at[k - 1],
+            recv_sem=share_recv.at[k - 1],
+            device_id={"loop": peer(k)},
+            device_id_type=pl.DeviceIdType.MESH,
+        )
+
+    for k in range(1, groups):
+        share_copy(k).start()
+    shares[me] = packed[me]
+    lax.fori_loop(0, pairs, sent, 0)
+    for k in range(1, groups):
+        share_copy(k).wait()
+    total = shares[0]
+    for g in range(1, groups):
+        total = total + shares[g]
+    packed[0] = total
+
+    def owned_copy(k):
+        rows = pl.ds(pl.multiple_of(above(k) * tile_rows, tile_rows), tile_rows)
+        return pltpu.make_async_remote_copy(
+            src_ref=packed.at[0, rows],
+            dst_ref=owned.at[floor],
+            send_sem=owned_send.at[k - 1],
+            recv_sem=owned_recv.at[k - 1],
+            device_id={"stack": above(k)},
+            device_id_type=pl.DeviceIdType.MESH,
+        )
+
+    for k in range(1, floors):
+        owned_copy(k).start()
+    owned[floor] = packed[0, pl.ds(pl.multiple_of(floor * tile_rows, tile_rows), tile_rows)]
+    fetch_lag.wait()
+    for k in range(1, floors):
+        owned_copy(k).wait()
+
+    tiles = []
+    per_tile = max(LANES // freq_dev, 1)
+    for start in range(0, floors, per_tile):
+        tile = owned[start]
+        for more in range(start + 1, start + per_tile):
+            tile = tile + owned[more]
+        tiles.append(tile)
+    spectrum = jnp.concatenate(tiles, 1)
+    freq_count = spectrum.shape[1]
+    slots = linear_ref.shape[0]
+    series[...] = jnp.zeros_like(series)
+    for k in range(slots):
+        re, im, phase_re, phase_im = (spectrum[4 * k + c : 4 * k + c + 1] for c in range(4))
+        coherence = phase_re * phase_re + phase_im * phase_im
+        series[k : k + 1, :freq_count] = re
+        series[k : k + 1, freq_count:] = im
+        series[slots + k : slots + k + 1, :freq_count] = re * coherence
+        series[slots + k : slots + k + 1, freq_count:] = im * coherence
+    parts = thirds(series[...])
+    corr = sum(
+        jnp.dot(part, lag_ref[n], preferred_element_type=jnp.float32)
+        for n in range(2)
+        for part in parts
+    )
+    power = jnp.mean(corr * corr, axis=1, keepdims=True)
+    corr = corr / jnp.sqrt(power + 1e-06)
+    linear_ref[...] = corr[:slots]
+    weighted_ref[...] = corr[slots : 2 * slots]
 
 
 def on_device(spectra, channel_loc, channel_valid, bin_owner):
@@ -246,10 +360,6 @@
     reps = LANES // bin_count
 
     x = spectra.reshape(loop_size, freqs, seg2, channels)
-    first = lax.axis_index("loop") * channels
-    late = channel_loc - 2 * (first + jnp.arange(channels, dtype=jnp.int32))
-    table = jnp.pad(jnp.stack([late, channel_valid]), ((0, 6), (0, 0)))
-
     chan = np.arange(nch)
     place = (chan % hop) * bin_count + chan // hop
     perm = jnp.asarray(place[:, None] == chan[None, :], jnp.bfloat16)
@@ -258,14 +368,54 @@
     same = (rep[:, None] == rep[None, :]) & (step[None, :] > step[:, None])
     base = jnp.asarray(np.stack([rep[:, None] < rep[None, :], same]), jnp.float32)
 
+    col = lane[:, None] % bin_count
+    row = np.arange(bin_count)[None, :]
+    to_bin = np.zeros((4, 3, LANES, 4, bin_count))
+    for c in range(4):
+        to_bin[c, 0, :, c] = col == row
+        to_bin[c, 1, :, c] = (col == bin_count - 1 - row) * (-1.0 if c % 2 else 1.0)
+        to_bin[c, 2, :, c] = col - 1 == row
+    to_bin = jnp.asarray(to_bin.reshape(12 * LANES, 4 * bin_count), jnp.bfloat16)
+
+    labels = jnp.arange(bin_count, dtype=jnp.int32)
+    same_owner = bin_owner[:, None] == bin_owner[None, :]
+    earlier = labels[None, :] < labels[:, None]
+    slot_rank = jnp.sum((same_owner & earlier).astype(jnp.int32), axis=1)
+    slot = bin_owner * BCAP + slot_rank
+    slots = BCAP // loop_size
+    tile_rows = max(4 * slots, 8)
+    line = np.arange(loop_size * stack_size * tile_rows)
+    owner = line // tile_rows % stack_size
+    number = line // (tile_rows * stack_size) * slots + line % tile_rows // 4
+    line_slot = np.where(line % tile_rows < 4 * slots, owner * BCAP + number, -1)
+    column = np.arange(4 * bin_count)
+    part_match = (line % 4)[:, None] == (column // bin_count)[None, :]
+    place = (
+        (jnp.tile(slot, 4)[None, :] == jnp.asarray(line_slot, jnp.int32)[:, None]) & part_match
+    ).astype(jnp.bfloat16)
+
+    freq_count = freq_dev * stack_size
+    matrix = lag_matrix(freq_count)
+    high = matrix.astype(jnp.bfloat16)
+    low = (matrix - high.astype(np.float32)).astype(jnp.bfloat16)
+    lags = jnp.asarray(np.stack([high, low]))
+
     whole = pl.BlockSpec(memory_space=pltpu.VMEM)
     far = pl.BlockSpec(memory_space=pl.ANY)
-    pair_sums = pl.pallas_call(
-        functools.partial(pair_kernel, bin_count, seg2),
-        out_shape=jax.ShapeDtypeStruct((freqs, 12, LANES), jnp.float32),
-        in_specs=[far, whole, far, whole],
-        out_specs=whole,
+    out = jax.ShapeDtypeStruct((slots, 2 * freq_count), jnp.float32)
+    linear, weighted = pl.pallas_call(
+        functools.partial(pair_kernel, bin_count, seg2, 3),
+        out_shape=(out, out),
+        in_specs=[far, whole, whole, far, whole, whole, whole, far],
+        out_specs=(whole, whole),
         scratch_shapes=[
+            pltpu.VMEM((8, LANES), jnp.int32),
+            pltpu.VMEM((12, LANES, LANES), jnp.float32),
+            pltpu.VMEM((loop_size, stack_size * tile_rows, LANES), jnp.float32),
+            pltpu.VMEM((loop_size, stack_size * tile_rows, LANES), jnp.float32),
+            pltpu.VMEM((stack_size, tile_rows, LANES), jnp.float32),
+            pltpu.VMEM(lags.shape, jnp.bfloat16),
+            pltpu.VMEM((8, 2 * freq_count), jnp.float32),
             pltpu.VMEM((loop_size, freqs, seg2, channels), jnp.bfloat16),
             pltpu.VMEM((loop_size, 8, LANES), jnp.int32),
             pltpu.VMEM((nch, nch), jnp.bfloat16),
@@ -277,51 +427,29 @@
             pltpu.SemaphoreType.DMA((freqs // 2, groups - 1)),
             pltpu.SemaphoreType.DMA((groups - 1,)),
             pltpu.SemaphoreType.DMA((groups - 1,)),
-            pltpu.SemaphoreType.DMA((3,)),
+            pltpu.SemaphoreType.DMA((groups - 1,)),
+            pltpu.SemaphoreType.DMA((groups - 1,)),
+            pltpu.SemaphoreType.DMA((stack_size - 1,)),
+            pltpu.SemaphoreType.DMA((stack_size - 1,)),
+            pltpu.SemaphoreType.DMA((4,)),
         ],
         compiler_params=pltpu.CompilerParams(
-            vmem_limit_bytes=48 * 2**20, collective_id=0, has_side_effects=True
+            vmem_limit_bytes=60 * 2**20, collective_id=0, has_side_effects=True
         ),
         cost_estimate=pl.CostEstimate(
             flops=freqs * nch * nch * seg2 * 2, bytes_accessed=8 * 2**20, transcendentals=0
         ),
-    )(x, table, perm, base)
-
-    labels = jnp.arange(bin_count, dtype=jnp.int32)
-    col = np.arange(LANES)[:, None] % bin_count
-    row = np.arange(bin_count)[None, :]
-    none = np.zeros((LANES, bin_count))
-    to_bin = np.concatenate(
-        [
-            np.concatenate([col == row, none], 1),
-            np.concatenate([none, col == bin_count - 1 - row], 1),
-            np.concatenate([col - 1 == row, none], 1),
-        ],
-        0,
-    ).astype(np.float32)
-    binned = jnp.dot(
-        pair_sums.reshape(freqs * 4, 3 * LANES),
-        jnp.asarray(to_bin),
-        precision=lax.Precision.HIGHEST,
-    ).reshape(freqs, 4, 2, bin_count)
-    sign = jnp.array([1.0, -1.0, 1.0, -1.0], jnp.float32)[None, :, None]
-    bins = binned[:, :, 0] + sign * binned[:, :, 1]
-
-    same_owner = bin_owner[:, None] == bin_owner[None, :]
-    earlier = labels[None, :] < labels[:, None]
-    slot_rank = jnp.sum((same_owner & earlier).astype(jnp.int32), axis=1)
-    slot = bin_owner * BCAP + slot_rank
-    placement = (
-        slot[:, None] == jnp.arange(BCAP * stack_size, dtype=jnp.int32)[None, :]
-    ).astype(jnp.float32)
-    packed = jnp.einsum("bs,fcb->scf", placement, bins, precision=lax.Precision.HIGHEST)
-    devices = stack_size * loop_size
-    packed = packed.reshape(devices, BCAP // loop_size, 4, freqs)
-    owned = lax.all_to_all(packed, ("stack", "loop"), 0, 0, tiled=True)
-    row_total = BCAP // loop_size
-    sums = owned.transpose(1, 2, 0, 3).reshape(row_total, 4, devices * freqs)
-    linear, weighted = finish(sums[:, 0], sums[:, 1], sums[:, 2], sums[:, 3])
-    return (linear.reshape(1, row_total, -1), weighted.reshape(1, row_total, -1))
+    )(
+        x,
+        channel_loc.reshape(1, channels),
+        channel_valid.reshape(1, channels),
+        perm,
+        base,
+        to_bin,
+        place,
+        lags,
+    )
+    return linear[None], weighted[None]
 
 
 def solution(mesh):

time: 70.9 us -> 65.2 us (0.920)
  Pallas kernels: 43.6 us -> 58.5 us
  blocking collectives: 13 us -> 0 us
  matrix products: 5.04 us -> 0 us
  local copies, waits for them, and re-layouts: 5.98 us -> 2.68 us
  other arithmetic: 2.3 us -> 3.06 us
    pallas_call x1, Pallas kernels: 43.6 us -> 58.5 us  [on_device(): pl.pallas_call(functools.partial(pair_kernel, bin_count, seg2, 3), out_sh...]
    all_to_all x1 -> x0, blocking collectives: 13 us -> none  [on_device(): owned = lax.all_to_all(packed, ('stack', 'loop'), 0, 0, tiled=True)]
    dot_general x3 -> x0, matrix products: 5.04 us -> none  [the longest x1 4.38 us: finish(): jnp.dot(jnp.concatenate([jnp.concatenate([linear_re, linear_im], 1), jnp....]
    unnamed x14 -> x2, local copies, waits for them, and re-layouts: 4.49 us -> 2.59 us
    convert_element_type x0 -> x1, other arithmetic: none -> 1.48 us  [on_device(): place = ((jnp.tile(slot, 4)[None, :] == jnp.asarray(line_slot, jnp.int32)...]
    another operation x2 -> x0, other arithmetic: 1.32 us -> none  [on_device(): table = jnp.pad(jnp.stack([late, channel_valid]), ((0, 6), (0, 0)))]
    reshape x3 -> x0, local copies, waits for them, and re-layouts: 0.79 us -> none  [the longest x1 0.62 us: on_device(): weighted.reshape(1, row_total, -1)]
    reduce_sum x1, other arithmetic: 0.18 us -> 0.91 us  [on_device(): slot_rank = jnp.sum((same_owner & earlier).astype(jnp.int32), axis=1)]
where the time goes in v2:
time: 65.2 us; the launch traced here: 64.9 us
  Pallas kernels  58.5 us (90%)
  other arithmetic  3.06 us (5%)
  local copies, waits for them, and re-layouts  2.68 us (4%)
    pallas_call x1, Pallas kernels, on_device(): pl.pallas_call(functools.partial(pair_kernel, bin_count, seg2, 3), out_sh...  58.5 us
    unnamed x2, local copies, waits for them, and re-layouts  2.59 us
    convert_element_type x1, other arithmetic, on_device(): place = ((jnp.tile(slot, 4)[None, :] == jnp.asarray(line_slot, jnp.int32)...  1.48 us

profile of v2, /device:TPU:0, one launch (start us, length us, event | category | flops | bytes accessed | tf_op | source)
XLA Modules:
  0.0 64.9 jit_solution(3460970266240231860)
XLA Ops:
  0.6 0.9 %convert_reduce_fusion = s32[32]{0:T(128)S(1)} fusion(s32[32]{0:T(128)} %param.13), kind=kLoop, calls=%fused_computation.1 | loop fusion | flops 5088 | bytes 256 | tf_op jit(solution)/shard_map/reduce_sum | solution.py:383
  1.5 0.7 %multiply_add_fusion = s32[32]{0:T(128)S(1)} fusion(s32[32]{0:T(128)S(1)} %convert_reduce_fusion, s32[32]{0:T(128)} %param.13), kind=kLoop, calls=%fused_computation.4 | loop fusion | flops 64 | bytes 384 | tf_op jit(solution)/shard_map/add | solution.py:384
  2.2 0.1 eq.31
  2.3 1.5 %and_convert_fusion.place_ref = bf16[256,128]{1,0:T(8,128)(2,1)} fusion(pred[256,128]{1,0:T(32,128)(4,1)} %constant.20.clone, s32[128]{0:T(128)S(1)} %eq.31, s32[256]{0:T(256)} %constant.19.clone), kind=kLoop, calls=%fused_computation | loop fusion | flops 98304 | bytes 99840 | tf_op jit(solution)/shard_map/convert_element_type | solution.py:395
  3.8 58.5 %shard_map.113 = (f32[2,1024]{1,0:T(2,128)}, f32[2,1024]{1,0:T(2,128)}) custom-call(bf16[8,16,64,128]{3,2,1,0:T(8,128)(2,1)} %bitcast.5, s32[1,128]{1,0:T(1,128)} %bitcast.8, s32[1,128]{1,0:T(1,128)} %bitcast.9, bf16[1024,1024]{1,0:T(8,128)(2,1)} %constant.16.clone.perm_hbm, f32[2,128,128]{2,1,0:T(8,128)} %constant.17.clone.base_ref, ...), custom_call_target="tpu_custom_call" | custom-call | flops 2147483648 | bytes 8388608 | tf_op jit(solution)/shard_map/pallas_call | solution.py:406
  62.3 1.3 %copy.15 = f32[1,2,1024]{2,1,0:T(2,128)} copy(f32[1,2,1024]{2,1,0:T(2,128)} %bitcast.7) | data formatting | bytes 16384
  63.6 1.3 %copy.16 = f32[1,2,1024]{2,1,0:T(2,128)} copy(f32[1,2,1024]{2,1,0:T(2,128)} %bitcast.6) | data formatting | bytes 16384
  (1 shorter events, 0.0 us)
